TPU v7x, 32 devices: a whole 2x2x4 slice. The times are simulated.
32 devices in a mesh: ops: 4 (over x, core), sec: 8 (over z, y).
Axes of the slice: x: 2, y: 2, z: 4, core: 2. Of those that a mesh axis runs over, the one named last changes fastest.
Arguments:
- wavefunction: float32 [8, 256, 1024], P('sec', 'ops'), may hold values from -8 to 8
- left_ops: float32 [4, 8, 256, 256], P('ops', 'sec'), may hold values from -0.375 to 0.375
- right_ops: float32 [4, 256, 256], P('ops'), may hold values from -0.375 to 0.375
- site_ops: float32 [4, 4, 4], P('ops'), may hold values from -3 to 3
- pattern: int32 [4, 8], P('ops', 'sec'), may hold values 0 or 1
- sector_sizes: int32 [8], P('sec'), may hold values from 1 to 256, 1536 in all
- owner: int32 [4], P('ops'), may hold values from 0 to 3
- slot: int32 [4], P('ops'), may hold values from 0 to 1
Outputs:
- basis: float32 [8, 256, 1024], P('sec', 'ops')
- complementary: float32 [4, 2, 256, 256], P('ops', None, 'sec')
Inputs may be any that keep to these rules, and one draw needn't show every extreme that they name: `sector_sizes`: each sector has at least one live state; some sector has all 256.
All inputs are finite; a program needn't handle non-finite values. No bound on the sum of `pattern` or of `sector_sizes` on one device may be relied on, other than what follows from the above.
Results may differ from a plain program's by a relative error of at most 0.0003.
Values sent between devices are 32-bit elements; how exact they have to be, the bound alone decides.
A program may use at most 64 MiB of HBM per device.

v0:
```python
import jax
import jax.numpy as jnp
from jax import lax
from jax.sharding import PartitionSpec as P

SLOTS = 2


highest = lax.Precision.HIGHEST


def body(wavefunction, left_ops, right_ops, site_ops, pattern, sector_sizes, owner, slot):
    ops_count = lax.axis_size("ops")
    sec_count = lax.axis_size("sec")
    row_share = wavefunction.shape[1]
    states = row_share * ops_count
    width_all = wavefunction.shape[2]
    columns = width_all // 4
    pair_count = left_ops.shape[0]
    live_all = (jnp.arange(states, dtype=jnp.int32) < sector_sizes[0]).astype(jnp.float32)
    left_block = left_ops[:, 0] * pattern[:, 0][:, None, None].astype(jnp.float32)
    row_start = lax.axis_index("ops") * row_share
    portion = lax.all_gather(wavefunction, "ops", axis=1, tiled=True)
    number = portion.shape[1]
    source = (portion[0] * live_all[:, None]).reshape(number, 4, columns)
    mapped = jnp.einsum("mqc,kcd->kmqd", source, right_ops, precision=highest)
    mapped = jnp.einsum("kpq,kmqd->kmpd", site_ops, mapped, precision=highest)
    mixed_all = mapped.reshape(pair_count, number, width_all)
    total_rows = 4 * states * sec_count
    scale = jnp.sqrt(jnp.float32(total_rows))
    summed = jnp.einsum("kmn,knw->mw", left_block, mixed_all, precision=highest)
    summed = lax.psum(summed, "ops")
    flat = (summed * live_all[:, None]).reshape(states * 4, columns)
    local_gram = jnp.dot(flat.T, flat, precision=highest, preferred_element_type=jnp.float32)
    gram = lax.psum(local_gram, "sec")
    factor = jnp.linalg.cholesky(gram)
    ortho_full = jax.scipy.linalg.solve_triangular(factor, flat.T, lower=True).T
    ortho_full = ortho_full.reshape(states, width_all)
    ortho_share = lax.dynamic_slice_in_dim(ortho_full, row_start, row_share, 0)
    basis = (ortho_share * scale).reshape(1, row_share, width_all)
    frame = ortho_full.reshape(states, 4, columns)
    moved = jnp.einsum("kmn,nqd->kmqd", left_block, frame, precision=highest)
    moved = jnp.einsum("kpq,kmqd->kmpd", site_ops, moved, precision=highest)
    renorm = jnp.einsum("mpc,kmpd->kcd", frame, moved, precision=highest)
    sector_sum = lax.psum_scatter(renorm, "sec", scatter_dimension=1, tiled=True)
    target = owner * SLOTS + slot
    select = (target[:, None] == jnp.arange(ops_count * SLOTS, dtype=jnp.int32)[None, :]).astype(
        jnp.float32
    )
    routed = jnp.einsum("kj,kcd->jcd", select, sector_sum, precision=highest)
    routed = routed.reshape(ops_count, SLOTS, sector_sum.shape[1], columns)
    complementary = lax.psum_scatter(routed, "ops", scatter_dimension=0, tiled=True)
    return (basis, complementary)


def solution(mesh):
    placed = (
        P("sec", "ops", None),
        P("ops", "sec", None, None),
        P("ops", None, None),
        P("ops", None, None),
        P("ops", "sec"),
        P("sec"),
        P("ops"),
        P("ops"),
    )
    return jax.shard_map(
        body,
        mesh=mesh,
        in_specs=placed,
        out_specs=(P("sec", "ops", None), P("ops", None, "sec", None)),
        check_vma=False,
    )
```

profile of v0, /device:TPU:0, one launch (start us, length us, event | category | flops | bytes accessed | tf_op | source)
XLA Modules:
  0.0 318.0 jit_solution(4397378280406869659)
XLA Ops:
  7.2 0.0 copy-start
  7.2 0.0 all-gather.2.cloned.1.call-start
  7.2 0.7 all-gather.2.cloned.1.call-update
  7.9 0.0 all-reduce.6.cloned.1.call-start
  9.3 19.8 %all-gather.2.cloned.1.call-done = f32[1,256,1024]{2,1,0:T(8,128)} async-done(((f32[1,64,1024]{2,1,0:T(8,128)}), f32[1,256,1024]{2,1,0:T(8,128)}) %all-gather.2.cloned.1.call-update) | async-done | bytes 1048592 | tf_op jit(solution)/shard_map/all_gather | solution.py:23
  29.0 1.4 broadcast_multiply_fusion.1
  30.4 0.5 mul.56
  30.9 0.0 copy-done
  30.9 0.0 copy-start.3
  30.9 1.0 fusion.4
  31.9 0.0 copy-done.3
  31.9 2.5 fusion.2
  34.4 0.0 copy-start.1
  34.4 0.2 copy.36
  34.7 0.7 copy-done.1
  35.4 2.1 fusion.14
  37.4 0.0 all-reduce.6.cloned.1.call-update
  37.5 0.0 all-reduce.8.cloned.1.call-start
  37.5 36.2 %all-reduce.6.cloned.1.call-done = f32[256,1024]{1,0:T(8,128)} async-done(((f32[256,1024]{1,0:T(8,128)}), f32[256,1024]{1,0:T(8,128)}) %all-reduce.6.cloned.1.call-update) | async-done | bytes 1048592 | tf_op jit(solution)/shard_map/psum | solution.py:32
  73.7 1.4 broadcast_multiply_fusion
  75.1 0.3 reshape.112
  75.4 2.5 fusion.28
  77.9 0.0 all-reduce.8.cloned.1.call-update
  77.9 0.2 all-reduce.10.cloned.1.call-start
  78.2 0.3 copy.26
  78.5 70.5 %all-reduce.8.cloned.1.call-done = f32[256,256]{0,1:T(8,128)} async-done(((f32[256,256]{0,1:T(8,128)}), f32[256,256]{0,1:T(8,128)}) %all-reduce.8.cloned.1.call-update) | async-done | bytes 262160 | tf_op jit(solution)/shard_map/psum | solution.py:35
  149.0 1.1 copy.25
  150.2 0.0 copy-done.2
  150.3 11.7 %cholesky.50 = f32[128,128]{1,0:T(8,128)S(1)} custom-call(f32[128,128]{1,0:T(8,128)S(1)} %cholesky.118), custom_call_target="Cholesky" | custom-call | tf_op jit(solution)/shard_map/jit(cholesky)/cholesky | solution.py:36
  162.0 9.8 %custom-call.15 = f32[1,128,128]{1,2,0:T(8,128)S(1)} custom-call(f32[1,128,128]{2,1,0:T(8,128)S(1)} %get-tuple-element.23), custom_call_target="InvertDiagBlocksLowerTriangular" | custom-call | tf_op jit(solution)/shard_map/jit(cholesky)/cholesky | solution.py:36
  171.8 0.2 constant_dynamic-update-slice_fusion
  172.1 0.3 convolution_subtract_fusion.1
  172.3 11.7 %cholesky.105 = f32[128,128]{1,0:T(8,128)S(1)} custom-call(f32[128,128]{1,0:T(8,128)S(1)} %convolution_subtract_fusion.1), custom_call_target="Cholesky" | custom-call | tf_op jit(solution)/shard_map/jit(cholesky)/cholesky | solution.py:36
  184.1 0.7 compare_reduce_fusion
  186.1 0.1 triangular_solve.57
  186.2 4.1 %while.1 = (s32[]{:T(128)}, f32[256,256]{1,0:T(8,128)S(1)}, s32[2,2]{1,0:T(2,128)S(1)}, f32[2,128,128]{2,1,0:T(8,128)S(1)}, s32[]{:T(128)}) while((s32[]{:T(128)}, f32[256,256]{1,0:T(8,128)S(1)}, s32[2,2]{1,0:T(2,128)S(1)}, f32[2,128,128]{2,1,0:T(8,128)S(1)}, s32[]{:T(128)}) %tuple.27), condition=%wide.while_cond, body=%wide.while_body.sunk | while | flops 2 | bytes 131189 | solution.py:37
  186.4 0.6 fusion.37
  186.9 1.4 bitcast_dynamic-update-slice_fusion.2
  188.3 0.6 fusion.37
  188.9 1.4 bitcast_dynamic-update-slice_fusion.2
  190.3 19.7 %custom-call.16 = f32[2,128,128]{1,2,0:T(8,128)S(1)} custom-call(f32[2,128,128]{2,1,0:T(8,128)S(1)} %get-tuple-element.9), custom_call_target="InvertDiagBlocksLowerTriangular" | custom-call | tf_op jit(solution)/shard_map/jit(_solve_triangular)/triangular_solve | solution.py:37
  210.0 0.6 fusion.9
  210.6 0.6 convolution_subtract_fusion
  211.2 0.6 fusion.21
  211.9 0.1 maximum_bitcast_fusion
  212.0 0.3 copy.27
  212.3 0.3 reshape_reshape.3
  212.6 1.1 fusion.7
  213.8 2.5 convolution_bitcast_fusion
  216.3 2.0 convolution_bitcast_fusion.1
  218.3 0.8 copy.33
  219.1 0.0 all-reduce.10.cloned.1.call-update
  219.1 0.0 reduce-scatter.2.cloned.1.call-start
  219.2 0.0 copy-start.4
  219.2 0.6 copy-done.4
  219.8 0.6 dynamic-slice.3
  222.4 0.1 reshape.137
  222.4 66.7 %all-reduce.10.cloned.1.call-done = f32[1,256,256]{2,0,1:T(1,128)} async-done(((f32[1,256,256]{2,0,1:T(1,128)}), f32[1,256,256]{2,0,1:T(1,128)}) %all-reduce.10.cloned.1.call-update) | async-done | bytes 262160
  289.1 0.8 constant_dynamic-slice_fusion.1
  289.9 0.8 broadcast_multiply_fusion.2
  290.7 0.0 reduce-scatter.2.cloned.1.call-update
  290.7 0.3 reshape.113
  291.0 0.7 multiply_bitcast_fusion
  291.7 19.8 %reduce-scatter.2.cloned.1.call-done = f32[1,2,32,256]{3,2,1,0:T(8,128)} async-done(((f32[4,2,32,256]{3,2,1,0:T(8,128)}), f32[1,2,32,256]{3,2,1,0:T(8,128)}) %reduce-scatter.2.cloned.1.call-update) | async-done | bytes 65552 | tf_op jit(solution)/shard_map/reduce_scatter | solution.py:52
  (14 shorter events, 0.2 us)
Async XLA Ops:
  7.2 23.7 %copy-start = (f32[1,256,256]{2,1,0:T(8,128)S(1)}, f32[1,256,256]{2,1,0:T(8,128)}, u32[]{:S(2)}) copy-start(f32[1,256,256]{2,1,0:T(8,128)} %param.10) | copy-start | bytes 786436
  7.2 21.8 %all-gather.2.cloned.1.call-start = ((), (), s32[]{:S(2)}) async-start(), calls=%async_computation.1 | async-start | bytes 1310720 | tf_op jit(solution)/shard_map/all_gather | solution.py:23
  7.9 65.8 %all-reduce.6.cloned.1.call-start = ((), (), s32[]{:S(2)}) async-start(), calls=%async_computation.2 | async-start | bytes 2097152 | tf_op jit(solution)/shard_map/psum | solution.py:32
  30.9 1.0 copy-start.3
  34.4 1.0 copy-start.1
  37.5 111.6 %all-reduce.8.cloned.1.call-start = ((), (), s32[]{:S(2)}) async-start(), calls=%async_computation.3 | async-start | bytes 524288 | tf_op jit(solution)/shard_map/psum | solution.py:35
  77.9 211.2 %all-reduce.10.cloned.1.call-start = ((), (), s32[]{:S(2)}) async-start(), calls=%async_computation.5 | async-start | bytes 524288
  149.0 1.2 copy-start.2
  219.1 92.4 %reduce-scatter.2.cloned.1.call-start = ((), (), s32[]{:S(2)}) async-start(), calls=%async_computation.4 | async-start | bytes 327680 | tf_op jit(solution)/shard_map/reduce_scatter | solution.py:52
  219.2 0.7 copy-start.4
Sparse Core Ops, SparseCore 0:
  9.6 19.4 all-gather.1
  37.6 36.0 all-reduce.5
  78.0 70.9 all-reduce.7
  219.2 69.8 all-reduce.9
  292.1 19.3 reduce-scatter.1
where the time goes:
time: 318 us
  waiting for transfers between devices  214 us (67%)
  other arithmetic  58.1 us (18%)
  between operations  18.6 us (6%)
  matrix products  16 us (5%)
  local copies, waits for them, and re-layouts  11.1 us (3%)
    psum x1, waiting for transfers between devices, body(): gram = lax.psum(local_gram, 'sec')  70.5 us
    unnamed x6, waiting for transfers between devices  67.4 us
    psum x1, waiting for transfers between devices, body(): summed = lax.psum(summed, 'ops')  36.2 us
    another operation x6, other arithmetic, body(): factor = jnp.linalg.cholesky(gram)  34 us
    all_gather x1, waiting for transfers between devices, body(): portion = lax.all_gather(wavefunction, 'ops', axis=1, tiled=True)  19.8 us
    reduce_scatter x1, waiting for transfers between devices, body(): lax.psum_scatter(routed, 'ops', scatter_dimension=0, tiled=True)  19.8 us
    another operation x3, other arithmetic, body(): ortho_full = jax.scipy.linalg.solve_triangular(factor, flat.T, lower=True).T  19.7 us
  transfers between devices with their start and end apart: 5, of which 5 were waited for; matrix products, arithmetic and copies ran while one was open for 1% of the time, Pallas kernels for 0%

commit v1 on v0

v1 whole, which is shorter than its diff:
```python
import functools

import jax
import jax.numpy as jnp
from jax import lax
from jax.experimental import pallas as pl
from jax.experimental.pallas import tpu as pltpu
from jax.sharding import PartitionSpec as P

SLOTS = 2
SITE = 4
HIGHEST = lax.Precision.HIGHEST
HIGH = lax.Precision.HIGH
MESH = pl.DeviceIdType.MESH
VM = pl.BlockSpec(memory_space=pltpu.VMEM)
SM = pl.BlockSpec(memory_space=pltpu.SMEM)
LIMIT = 40 * 1024 * 1024


def remote(src, dst, send, recv, dev):
    return pltpu.make_async_remote_copy(
        src_ref=src, dst_ref=dst, send_sem=send, recv_sem=recv, device_id=dev, device_id_type=MESH
    )


def greet(devs):
    barrier = pltpu.get_barrier_semaphore()
    for dev in devs:
        pl.semaphore_signal(barrier, inc=1, device_id=dev, device_id_type=MESH)
    pl.semaphore_wait(barrier, len(devs))


def dot(a, b, dims, precision):
    return lax.dot_general(a, b, (dims, ((), ())), precision=precision, preferred_element_type=jnp.float32)


NN = ((1,), (0,))
NT = ((1,), (1,))
TN = ((0,), (0,))


def gather_kernel(n, count, *refs):
    ins, outs = refs[:count], refs[count:2 * count]
    send, recv, local = refs[2 * count:]
    me = lax.axis_index("ops")
    chips = n // 2
    core = lax.rem(me, 2)
    chip = me // 2
    mate = {"ops": chip * 2 + 1 - core}
    away = [{"ops": lax.rem(chip + d, chips) * 2 + core} for d in range(1, chips)]
    back = [lax.rem(chip + chips - d, chips) * 2 + core for d in range(1, chips)]
    greet(away + [mate])
    direct = chips - 1
    started = []
    for a in range(count):
        for i, dev in enumerate(away):
            c = remote(ins[a], outs[a].at[me], send.at[a, i], recv.at[a, i], dev)
            c.start()
            started.append(c)
        c = remote(ins[a], outs[a].at[me], send.at[a, direct], recv.at[a, direct], mate)
        c.start()
        started.append(c)
    own = [pltpu.make_async_copy(ins[a], outs[a].at[me], local.at[a]) for a in range(count)]
    for c in own:
        c.start()
    relays = []
    for a in range(count):
        for i, src in enumerate(back):
            remote(ins[a], outs[a].at[src], send.at[a, i], recv.at[a, i], away[i]).wait_recv()
            c = remote(outs[a].at[src], outs[a].at[src], send.at[a, chips + i], recv.at[a, chips + i], mate)
            c.start()
            relays.append(c)
    for c in own:
        c.wait()
    for a in range(count):
        remote(ins[a], outs[a].at[me], send.at[a, direct], recv.at[a, direct], mate).wait_recv()
    for c in relays:
        c.wait_recv()
    for c in started + relays:
        c.wait_send()


def gather(n, arrays):
    count = len(arrays)
    return pl.pallas_call(
        functools.partial(gather_kernel, n, count),
        out_shape=[jax.ShapeDtypeStruct((n,) + a.shape, a.dtype) for a in arrays],
        in_specs=[VM] * count,
        out_specs=[VM] * count,
        scratch_shapes=[
            pltpu.SemaphoreType.DMA((count, n)),
            pltpu.SemaphoreType.DMA((count, n)),
            pltpu.SemaphoreType.DMA((count,)),
        ],
        compiler_params=pltpu.CompilerParams(collective_id=0, has_side_effects=True, vmem_limit_bytes=LIMIT),
    )(*arrays)


def sigma_kernel(size_ref, meta_ref, psi_ref, left_ref, right_ref, x_ref, gram_ref, mixed):
    rows, width = psi_ref.shape
    cols = width // SITE
    live = lax.broadcasted_iota(jnp.int32, (rows, cols), 0) < size_ref[0]
    total = jnp.zeros((rows, width), jnp.float32)
    for k in range(left_ref.shape[0]):
        mapped = [
            dot(jnp.where(live, psi_ref[:, q * cols:(q + 1) * cols], 0.0), right_ref[k], NN, HIGH)
            for q in range(SITE)
        ]
        for p in range(SITE):
            mix = mapped[0] * meta_ref[k, p * SITE]
            for q in range(1, SITE):
                mix += mapped[q] * meta_ref[k, p * SITE + q]
            mixed[:, p * cols:(p + 1) * cols] = mix
        total += dot(left_ref[k] * meta_ref[k, SITE * SITE], mixed[...], NN, HIGH)
    gram = jnp.zeros((cols, cols), jnp.float32)
    for p in range(SITE):
        part = jnp.where(live, total[:, p * cols:(p + 1) * cols], 0.0)
        x_ref[:, p * cols:(p + 1) * cols] = part
        gram += dot(part, part, TN, HIGHEST)
    gram_ref[...] = gram


def reduce_kernel(n, m, wide, gram_ref, out_ref, held, send, recv, send2, recv2):
    o, s = lax.axis_index("ops"), lax.axis_index("sec")
    size = gram_ref.shape[0]
    rows = held.shape[1]
    others = [(a, b) for a in range(n if wide else 1) for b in range(m) if a or b]
    devs = [{"ops": lax.rem(o + a, n), "sec": lax.rem(s + b, m)} for a, b in others]

    def place(a, b):
        at = a * m + b if wide else b
        return pl.ds(pl.multiple_of(at * rows, rows), rows)

    greet(devs)
    first = []
    for b in range(1, m):
        to = lax.rem(s + b, m)
        c = remote(gram_ref.at[place(o, to)], held.at[b - 1], send.at[b - 1], recv.at[b - 1], {"sec": to})
        c.start()
        first.append(c)
    mine = place(o, s)
    total = gram_ref[mine, :]
    for b in range(1, m):
        first[b - 1].wait_recv()
        total += held[b - 1]
    out_ref[mine, :] = total
    second = []
    for i, dev in enumerate(devs):
        c = remote(out_ref.at[mine], out_ref.at[mine], send2.at[i], recv2.at[i], dev)
        c.start()
        second.append(c)
    for i, (a, b) in enumerate(others):
        at = place(lax.rem(o + n - a, n), lax.rem(s + m - b, m))
        remote(out_ref.at[at], out_ref.at[at], send2.at[i], recv2.at[i], devs[i]).wait_recv()
    for c in first + second:
        c.wait_send()


def reduce_gram(n, m, gram):
    size = gram.shape[0]
    wide = size % (8 * n * m) == 0
    rows = size // (n * m) if wide else size // m
    peers = (n if wide else 1) * m - 1
    return pl.pallas_call(
        functools.partial(reduce_kernel, n, m, wide),
        out_shape=jax.ShapeDtypeStruct(gram.shape, jnp.float32),
        in_specs=[VM],
        out_specs=VM,
        scratch_shapes=[
            pltpu.VMEM((m - 1, rows, size), jnp.float32),
            pltpu.SemaphoreType.DMA((m - 1,)),
            pltpu.SemaphoreType.DMA((m - 1,)),
            pltpu.SemaphoreType.DMA((peers,)),
            pltpu.SemaphoreType.DMA((peers,)),
        ],
        compiler_params=pltpu.CompilerParams(collective_id=1, has_side_effects=True, vmem_limit_bytes=LIMIT),
    )(gram)


def small_inverse(block):
    b = block.shape[0]
    eye = (
        lax.broadcasted_iota(jnp.int32, (b, b), 0) == lax.broadcasted_iota(jnp.int32, (b, b), 1)
    ).astype(jnp.float32)
    work = jnp.concatenate([block, eye], axis=1)
    parts = [work[t * 8:(t + 1) * 8] for t in range(b // 8)]
    under = lax.broadcasted_iota(jnp.int32, (8, 1), 0)
    for j in range(b):
        t0, r = divmod(j, 8)
        row = parts[t0][r:r + 1, :]
        ratio = row / row[:, j:j + 1]
        for t in range(t0, b // 8):
            col = parts[t][:, j:j + 1]
            if t == t0:
                if r == 7:
                    continue
                col = jnp.where(under > r, col, 0.0)
            parts[t] = parts[t] - col * ratio
    work = jnp.concatenate(parts, axis=0)
    pivot = jnp.sum(work[:, :b] * eye, axis=1, keepdims=True)
    return work[:, b:] / jnp.sqrt(pivot)


def finish_kernel(scale, site_ref, gram_ref, x_ref, left_ref, basis_ref, renorm_ref, work, inverse, frame, mixed):
    cols = gram_ref.shape[0]
    rows = basis_ref.shape[0]
    block = 64
    work[:, :cols] = gram_ref[...]
    work[:, cols:] = (
        lax.broadcasted_iota(jnp.int32, (cols, cols), 0) == lax.broadcasted_iota(jnp.int32, (cols, cols), 1)
    ).astype(jnp.float32)
    for at in range(0, cols, block):
        end = at + block
        small = small_inverse(work[at:end, at:end])
        strip = dot(small, work[at:end, :], NN, HIGHEST)
        inverse[at:end, :] = strip[:, cols:]
        if end < cols:
            work[end:, :] -= dot(strip[:, end:cols], strip, TN, HIGHEST)
    for p in range(SITE):
        part = slice(p * cols, (p + 1) * cols)
        frame[:, part] = dot(x_ref[:, part], inverse[...], NT, HIGH)
    start = pl.multiple_of(lax.axis_index("ops") * rows, rows)
    basis_ref[...] = frame[pl.ds(start, rows), :] * scale
    for k in range(left_ref.shape[0]):
        mixed[...] = dot(left_ref[k] * site_ref[k, SITE * SITE], frame[...], NN, HIGH)
        moved = [mixed[:, q * cols:(q + 1) * cols] for q in range(SITE)]
        total = jnp.zeros((cols, cols), jnp.float32)
        for p in range(SITE):
            mix = moved[0] * site_ref[k, p * SITE]
            for q in range(1, SITE):
                mix += moved[q] * site_ref[k, p * SITE + q]
            total += dot(frame[:, p * cols:(p + 1) * cols], mix, TN, HIGH)
        renorm_ref[k] = total


def route_kernel(n, m, weight_ref, renorm_ref, out_ref, held, summed, send, recv, send2, recv2):
    o, s = lax.axis_index("ops"), lax.axis_index("sec")
    pairs, size, width = renorm_ref.shape
    rows = held.shape[2]
    secs = [{"sec": lax.rem(s + b, m)} for b in range(1, m)]
    opses = [{"ops": lax.rem(o + a, n)} for a in range(1, n)]
    greet(secs + opses)

    def place(b):
        return pl.ds(pl.multiple_of(b * rows, rows), rows)

    first = []
    for b in range(1, m):
        to = lax.rem(s + b, m)
        c = remote(renorm_ref.at[:, place(to)], held.at[b - 1], send.at[b - 1], recv.at[b - 1], {"sec": to})
        c.start()
        first.append(c)
    total = renorm_ref[:, place(s), :]
    for b in range(1, m):
        first[b - 1].wait_recv()
        total += held[b - 1]
    summed[0] = total
    second = []
    for a in range(1, n):
        c = remote(summed.at[0], summed.at[a], send2.at[a - 1], recv2.at[a - 1], opses[a - 1])
        c.start()
        second.append(c)
    out = [jnp.zeros((rows, width), jnp.float32) for _ in range(SLOTS)]
    for a in range(n):
        if a:
            second[a - 1].wait_recv()
        for k in range(pairs):
            term = summed[a, k]
            for j in range(SLOTS):
                out[j] += term * weight_ref[a * pairs + k, j]
    for j in range(SLOTS):
        out_ref[j] = out[j]
    for c in first + second:
        c.wait_send()


def body(n, m, wavefunction, left_ops, right_ops, site_ops, pattern, sector_sizes, owner, slot):
    row_share, width = wavefunction.shape[1:]
    pairs = left_ops.shape[0]
    cols = width // SITE
    states = row_share * n
    f32 = jnp.float32
    meta = jnp.concatenate(
        [
            site_ops.reshape(pairs, SITE * SITE),
            pattern[:, :1].astype(f32),
            owner[:, None].astype(f32),
            slot[:, None].astype(f32),
        ],
        axis=1,
    )
    meta = jnp.pad(meta, ((0, 0), (0, 128 - meta.shape[1])))
    left = left_ops[:, 0]
    psi, left_all, right_all, meta_all = gather(n, [wavefunction[0], left, right_ops, meta])
    meta_all = meta_all.reshape(n * pairs, 128)
    x, gram = pl.pallas_call(
        sigma_kernel,
        out_shape=[jax.ShapeDtypeStruct((states, width), f32), jax.ShapeDtypeStruct((cols, cols), f32)],
        in_specs=[SM, SM, VM, VM, VM],
        out_specs=[VM, VM],
        scratch_shapes=[pltpu.VMEM((states, width), f32)],
        compiler_params=pltpu.CompilerParams(vmem_limit_bytes=LIMIT),
    )(
        sector_sizes,
        meta_all[:, :SITE * SITE + 1],
        psi.reshape(states, width),
        left_all.reshape(n * pairs, states, states),
        right_all.reshape(n * pairs, cols, cols),
    )
    gram = reduce_gram(n, m, gram)
    scale = float(SITE * states * m) ** 0.5
    basis, renorm = pl.pallas_call(
        functools.partial(finish_kernel, scale),
        out_shape=[
            jax.ShapeDtypeStruct((row_share, width), f32),
            jax.ShapeDtypeStruct((pairs, cols, cols), f32),
        ],
        in_specs=[SM, VM, VM, VM],
        out_specs=[VM, VM],
        scratch_shapes=[
            pltpu.VMEM((cols, 2 * cols), f32),
            pltpu.VMEM((cols, cols), f32),
            pltpu.VMEM((states, width), f32),
            pltpu.VMEM((states, width), f32),
        ],
        compiler_params=pltpu.CompilerParams(vmem_limit_bytes=LIMIT),
    )(meta[:, :SITE * SITE + 1], gram, x, left)
    me = lax.axis_index("ops")
    order = (me - jnp.arange(n, dtype=jnp.int32) + n) % n
    facts = meta_all.reshape(n, pairs, 128)[order].reshape(n * pairs, 128)[:, SITE * SITE + 1:SITE * SITE + 3]
    target = facts[:, 0] * SLOTS + facts[:, 1] - (me * SLOTS).astype(f32)
    weight = (target[:, None] == jnp.arange(SLOTS, dtype=f32)[None, :]).astype(f32)
    rows = cols // m
    complementary = pl.pallas_call(
        functools.partial(route_kernel, n, m),
        out_shape=jax.ShapeDtypeStruct((SLOTS, rows, cols), f32),
        in_specs=[SM, VM],
        out_specs=VM,
        scratch_shapes=[
            pltpu.VMEM((m - 1, pairs, rows, cols), f32),
            pltpu.VMEM((n, pairs, rows, cols), f32),
            pltpu.SemaphoreType.DMA((m - 1,)),
            pltpu.SemaphoreType.DMA((m - 1,)),
            pltpu.SemaphoreType.DMA((n - 1,)),
            pltpu.SemaphoreType.DMA((n - 1,)),
        ],
        compiler_params=pltpu.CompilerParams(collective_id=2, has_side_effects=True, vmem_limit_bytes=LIMIT),
    )(weight, renorm)
    return basis[None], complementary[None]


def solution(mesh):
    placed = (
        P("sec", "ops", None),
        P("ops", "sec", None, None),
        P("ops", None, None),
        P("ops", None, None),
        P("ops", "sec"),
        P("sec"),
        P("ops"),
        P("ops"),
    )
    return jax.shard_map(
        functools.partial(body, mesh.shape["ops"], mesh.shape["sec"]),
        mesh=mesh,
        in_specs=placed,
        out_specs=(P("sec", "ops", None), P("ops", None, "sec", None)),
        check_vma=False,
    )
```

time: 318 us -> 94.4 us (0.30)
  waiting for transfers between devices: 214 us -> 0 us
  Pallas kernels: 0 us -> 86.2 us
  other arithmetic: 58.1 us -> 0.44 us
  matrix products: 16 us -> 0 us
  between operations: 18.6 us -> 3.32 us
  local copies, waits for them, and re-layouts: 11.1 us -> 4.15 us
    psum x2 -> x0, waiting for transfers between devices: 107 us -> none  [the longest x1 70.5 us: body(): gram = lax.psum(local_gram, 'sec')]
    pallas_call x0 -> x5, Pallas kernels: none -> 86.2 us  [the longest x1 26.9 us: body(): pl.pallas_call(functools.partial(finish_kernel, scale), out_shape=[jax.Sh...]
    unnamed x6 -> x0, waiting for transfers between devices: 67.4 us -> none
    another operation x10 -> x0, other arithmetic: 53.7 us -> none  [the longest x6 34 us: body(): factor = jnp.linalg.cholesky(gram)]
    all_gather x1 -> x0, waiting for transfers between devices: 19.8 us -> none  [body(): portion = lax.all_gather(wavefunction, 'ops', axis=1, tiled=True)]
    reduce_scatter x1 -> x0, waiting for transfers between devices: 19.8 us -> none  [body(): lax.psum_scatter(routed, 'ops', scatter_dimension=0, tiled=True)]
    dot_general x7 -> x0, matrix products: 13.7 us -> none  [the longest x1 2.52 us: body(): jnp.dot(flat.T, flat, precision=highest, preferred_element_type=jnp.float32)]
    another operation x11 -> x0, local copies, waits for them, and re-layouts: 4.41 us -> none
  transfers between devices with their start and end apart: 5 -> 0, of which waited for: 5 -> 0; matrix products, arithmetic and copies ran while one was open for 1% -> 0% of each run, Pallas kernels for 0% -> 0%
where the time goes in v1:
time: 94.4 us; the launch traced here: 94.1 us
  Pallas kernels  86.2 us (91%)
  local copies, waits for them, and re-layouts  4.15 us (4%)
  between operations  3.32 us (4%)
    pallas_call x1, Pallas kernels, body(): pl.pallas_call(functools.partial(finish_kernel, scale), out_shape=[jax.Sh...  26.9 us
    pallas_call x1, Pallas kernels, gather(): pl.pallas_call(functools.partial(gather_kernel, n, count), out_shape=[jax...  22.6 us
    pallas_call x1, Pallas kernels, reduce_gram(): pl.pallas_call(functools.partial(reduce_kernel, n, m, wide), out_shape=ja...  16.9 us
    pallas_call x1, Pallas kernels, body(): pl.pallas_call(functools.partial(route_kernel, n, m), out_shape=jax.Shape...  12.4 us
    pallas_call x1, Pallas kernels, body(): pl.pallas_call(sigma_kernel, out_shape=[jax.ShapeDtypeStruct((states, wid...  7.36 us
    unnamed x11, local copies, waits for them, and re-layouts  3.5 us

profile of v1, /device:TPU:0, one launch (start us, length us, event | category | flops | bytes accessed | tf_op | source)
XLA Modules:
  0.0 94.1 jit_solution(8442624026959096427)
XLA Ops:
  0.6 0.0 copy-start.4
  1.3 0.0 copy-done.4
  1.3 0.1 reshape.76
  1.4 0.1 pad_maximum_fusion.site_ref
  3.4 0.1 select_maximum_fusion.refs_3_
  3.5 0.0 copy-start
  3.5 0.9 %copy-done = f32[1,1,256,256]{3,2,1,0:T(8,128)S(1)} copy-done((f32[1,1,256,256]{3,2,1,0:T(8,128)S(1)}, f32[1,1,256,256]{3,2,1,0:T(8,128)}, u32[]{:S(2)}) %copy-start) | copy-done | bytes 262168
  4.5 0.0 copy-start.2
  4.5 0.9 %copy-done.2 = f32[1,64,1024]{2,1,0:T(8,128)S(1)} copy-done((f32[1,64,1024]{2,1,0:T(8,128)S(1)}, f32[1,64,1024]{2,1,0:T(8,128)}, u32[]{:S(2)}) %copy-start.2) | copy-done | bytes 262168
  5.4 0.0 copy-start.3
  5.4 0.9 %copy-done.3 = f32[1,256,256]{2,1,0:T(8,128)S(1)} copy-done((f32[1,256,256]{2,1,0:T(8,128)S(1)}, f32[1,256,256]{2,1,0:T(8,128)}, u32[]{:S(2)}) %copy-start.3) | copy-done | bytes 262168
  6.4 22.6 %shard_map.95 = (f32[4,64,1024]{2,1,0:T(8,128)S(1)}, f32[4,1,256,256]{3,2,1,0:T(8,128)S(1)}, f32[4,1,256,256]{3,2,1,0:T(8,128)S(1)}, f32[4,1,128]{2,1,0:T(1,128)S(1)}) custom-call(f32[64,1024]{1,0:T(8,128)S(1)} %bitcast.19, f32[1,256,256]{2,1,0:T(8,128)S(1)} %bitcast.16, f32[1,256,256]{2,1,0:T(8,128)S(1)} %copy-done.3, f32[1,128]{1,0:T(1,128)S(1)} %select_maximum_fusion.refs_3_), custom_call_target="tpu_custom_call" | custom-call | tf_op jit(solution)/shard_map/pallas_call | solution.py:85
  29.0 7.4 %shard_map.96 = (f32[256,1024]{1,0:T(8,128)S(1)}, f32[256,256]{1,0:T(8,128)S(1)}) custom-call(s32[1]{0:T(128)S(6)} %copy.12.size_ref, f32[4,17]{1,0:T(4,128)S(1)} %bitcast.20, f32[256,1024]{1,0:T(8,128)S(1)} %bitcast.13, f32[4,256,256]{2,1,0:T(8,128)S(1)} %bitcast.14, f32[4,256,256]{2,1,0:T(8,128)S(1)} %bitcast.15), custom_call_target="tpu_custom_call" | custom-call | tf_op jit(solution)/shard_map/pallas_call | solution.py:296
  36.4 0.0 copy-start.1
  36.4 16.9 %shard_map.97.gram_ref = f32[256,256]{1,0:T(8,128)S(1)} custom-call(f32[256,256]{1,0:T(8,128)S(1)} %get-tuple-element.14.gram_ref), custom_call_target="tpu_custom_call" | custom-call | tf_op jit(solution)/shard_map/pallas_call | solution.py:164
  53.3 0.0 copy-done.1
  53.3 26.9 %shard_map.98 = (f32[64,1024]{1,0:T(8,128)}, f32[1,256,256]{2,1,0:T(8,128)S(1)}) custom-call(f32[1,17]{1,0:T(1,128)S(1)} %pad_maximum_fusion.site_ref, f32[256,256]{1,0:T(8,128)S(1)} %shard_map.97.gram_ref, f32[256,1024]{1,0:T(8,128)S(1)} %get-tuple-element.15.x_ref, f32[1,256,256]{2,1,0:T(8,128)S(1)} %bitcast.17), custom_call_target="tpu_custom_call" | custom-call | tf_op jit(solution)/shard_map/pallas_call | solution.py:312
  80.3 0.6 gather_fusion
  80.8 0.2 subtract_reduce_fusion
  81.0 0.1 fusion.weight_ref
  81.1 12.4 %shard_map.99 = f32[2,32,256]{2,1,0:T(8,128)S(1)} custom-call(f32[4,2]{1,0:T(4,128)S(1)} %fusion.weight_ref, f32[1,256,256]{2,1,0:T(8,128)S(1)} %get-tuple-element.17.renorm_ref), custom_call_target="tpu_custom_call" | custom-call | tf_op jit(solution)/shard_map/pallas_call | solution.py:334
  93.5 0.6 copy.15
  (2 shorter events, 0.0 us)
Async XLA Ops:
  0.6 0.7 copy-start.4
  3.5 1.0 %copy-start = (f32[1,1,256,256]{3,2,1,0:T(8,128)S(1)}, f32[1,1,256,256]{3,2,1,0:T(8,128)}, u32[]{:S(2)}) copy-start(f32[1,1,256,256]{3,2,1,0:T(8,128)} %param.9) | copy-start | bytes 786436
  4.5 0.9 %copy-start.2 = (f32[1,64,1024]{2,1,0:T(8,128)S(1)}, f32[1,64,1024]{2,1,0:T(8,128)}, u32[]{:S(2)}) copy-start(f32[1,64,1024]{2,1,0:T(8,128)} %param.8) | copy-start | bytes 786436
  5.4 0.9 %copy-start.3 = (f32[1,256,256]{2,1,0:T(8,128)S(1)}, f32[1,256,256]{2,1,0:T(8,128)}, u32[]{:S(2)}) copy-start(f32[1,256,256]{2,1,0:T(8,128)} %refs_2_.1) | copy-start | bytes 786436
  36.4 16.9 %copy-start.1 = (f32[1,1,256,256]{3,2,1,0:T(8,128)S(1)}, f32[1,1,256,256]{3,2,1,0:T(8,128)}, u32[]{:S(2)}) copy-start(f32[1,1,256,256]{3,2,1,0:T(8,128)} %param.9) | copy-start | bytes 786436

commit v2 on v0

v2 whole, which is shorter than its diff:
```python
import functools

import jax
import jax.numpy as jnp
from jax import lax
from jax.experimental import pallas as pl
from jax.experimental.pallas import tpu as pltpu
from jax.sharding import PartitionSpec as P

SLOTS = 2
SITE = 4
HIGHEST = lax.Precision.HIGHEST
HIGH = lax.Precision.HIGH
MESH = pl.DeviceIdType.MESH
VM = pl.BlockSpec(memory_space=pltpu.VMEM)
SM = pl.BlockSpec(memory_space=pltpu.SMEM)
ANY = pl.BlockSpec(memory_space=pl.ANY)
LIMIT = 48 * 1024 * 1024


def remote(src, dst, send, recv, dev):
    return pltpu.make_async_remote_copy(
        src_ref=src, dst_ref=dst, send_sem=send, recv_sem=recv, device_id=dev, device_id_type=MESH
    )


def greet(devs):
    barrier = pltpu.get_barrier_semaphore()
    for dev in devs:
        pl.semaphore_signal(barrier, inc=1, device_id=dev, device_id_type=MESH)
    pl.semaphore_wait(barrier, len(devs))


def dot(a, b, dims, precision):
    return lax.dot_general(a, b, (dims, ((), ())), precision=precision, preferred_element_type=jnp.float32)


NN = ((1,), (0,))
NT = ((1,), (1,))
TN = ((0,), (0,))


def small_inverse(block):
    b = block.shape[0]
    eye = (
        lax.broadcasted_iota(jnp.int32, (b, b), 0) == lax.broadcasted_iota(jnp.int32, (b, b), 1)
    ).astype(jnp.float32)
    work = jnp.concatenate([block, eye], axis=1)
    lanes = work.shape[1]
    count = b // 8
    parts = [work[t * 8:(t + 1) * 8] for t in range(count)]
    under = lax.broadcasted_iota(jnp.int32, (8, lanes), 0)
    for g in range(count):
        spread = [
            [jnp.broadcast_to(parts[t][:, g * 8 + i:g * 8 + i + 1], (8, lanes)) for i in range(8)]
            for t in range(g, count)
        ]
        rows = parts[g]
        for r in range(8):
            inv = 1.0 / spread[0][r][r:r + 1, :]
            ratio = rows[r:r + 1, :] * inv
            steps = [spread[0][i][r:r + 1, :] * inv for i in range(r + 1, 8)]
            for t in range(count - g):
                col = spread[t][r]
                if t == 0:
                    if r == 7:
                        continue
                    col = jnp.where(under > r, col, 0.0)
                    rows = rows - col * ratio
                else:
                    parts[g + t] = parts[g + t] - col * ratio
                for i in range(r + 1, 8):
                    spread[t][i] = spread[t][i] - col * steps[i - r - 1]
        parts[g] = rows
    work = jnp.concatenate(parts, axis=0)
    pivot = jnp.sum(work[:, :b] * eye, axis=1, keepdims=True)
    return work[:, b:] / jnp.sqrt(pivot)


def kernel(
    n, m, wide, scale, size_ref, meta_in, psi_in, left_in, right_in, basis_ref, out_ref,
    meta, psi, left, right, mixed, x, gram, whole, held, work, inverse, frame, renorm, taken, summed,
    send, recv, local, send1, recv1, send2, recv2, send3, recv3, send4, recv4,
):
    o, s = lax.axis_index("ops"), lax.axis_index("sec")
    pairs = left_in.shape[0]
    row_share, width = psi_in.shape
    states = row_share * n
    cols = width // SITE
    others = [(a, b) for a in range(n) for b in range(m) if (a or b) and (wide or not a or not b)]
    devs = [{"ops": lax.rem(o + a, n), "sec": lax.rem(s + b, m)} for a, b in others]
    greet(devs)

    ins, outs = (meta_in, psi_in, right_in, left_in), (meta, psi, right, left)
    chips = n // 2
    core = lax.rem(o, 2)
    chip = o // 2
    direct = chips - 1
    mate_at = chip * 2 + 1 - core
    mate = {"ops": mate_at, "sec": s}
    away = [{"ops": lax.rem(chip + d, chips) * 2 + core, "sec": s} for d in range(1, chips)]
    back = [lax.rem(chip + chips - d, chips) * 2 + core for d in range(1, chips)]
    far = [lax.rem(chip + chips - d, chips) * 2 + 1 - core for d in range(1, chips)]
    pending = []

    def begin(c):
        c.start()
        pending.append(c)
        return c

    own = [pltpu.make_async_copy(ins[a], outs[a].at[o], local.at[a]) for a in range(4)]
    for a in range(4):
        for i, dev in enumerate(away):
            begin(remote(ins[a], outs[a].at[o], send.at[a, i], recv.at[a, i], dev))
        begin(remote(ins[a], outs[a].at[o], send.at[a, direct], recv.at[a, direct], mate))
        own[a].start()

    def relay(a):
        for i, src in enumerate(back):
            remote(ins[a], outs[a].at[src], send.at[a, i], recv.at[a, i], away[i]).wait_recv()
            begin(remote(outs[a].at[src], outs[a].at[src], send.at[a, chips + i], recv.at[a, chips + i], mate))

    def from_mate(a):
        remote(ins[a], outs[a].at[mate_at], send.at[a, direct], recv.at[a, direct], mate).wait_recv()

    def from_far(a, i):
        remote(outs[a].at[far[i]], outs[a].at[far[i]], send.at[a, chips + i], recv.at[a, chips + i], mate).wait_recv()

    for a in (0, 1):
        own[a].wait()
        from_mate(a)
        relay(a)
        for i in range(direct):
            from_far(a, i)

    live = lax.broadcasted_iota(jnp.int32, (states, width), 0) < size_ref[0]
    x[...] = jnp.where(live, psi[...].reshape(states, width), 0.0)
    order = [o, mate_at] + back + far

    def scalar(at, k, i):
        return meta[at, k:k + 1, i:i + 1]

    def mix_site(parts, at, k, p):
        total = parts[0] * scalar(at, k, p * SITE)
        for q in range(1, SITE):
            total += parts[q] * scalar(at, k, p * SITE + q)
        return total

    def map_right(i):
        for k in range(pairs):
            mapped = [
                dot(x[:, q * cols:(q + 1) * cols], right[order[i], k], NN, HIGH) for q in range(SITE)
            ]
            for p in range(SITE):
                mixed[i * pairs + k, :, p * cols:(p + 1) * cols] = mix_site(mapped, order[i], k, p)

    def apply_left(i, total):
        for k in range(pairs):
            block = left[order[i], k] * scalar(order[i], k, SITE * SITE)
            total = total + dot(block, mixed[i * pairs + k], NN, HIGH)
        return total

    def arrive(a, i):
        if i == 0:
            own[a].wait()
        elif i == 1:
            from_mate(a)
        elif i < 2 + direct:
            if i == 2:
                relay(a)
        else:
            from_far(a, i - 2 - direct)

    for i in range(n):
        arrive(2, i)
        map_right(i)
    total = jnp.zeros((states, width), jnp.float32)
    for i in range(n):
        arrive(3, i)
        total = apply_left(i, total)
    x[...] = jnp.where(live, total, 0.0)
    gram[...] = sum(dot(x[:, p * cols:(p + 1) * cols], x[:, p * cols:(p + 1) * cols], TN, HIGHEST) for p in range(SITE))

    rows = held.shape[1]

    def place(a, b):
        at = a * m + b if wide else b
        return pl.ds(pl.multiple_of(at * rows, rows), rows)

    first = []
    for b in range(1, m):
        to = lax.rem(s + b, m)
        dev = {"ops": o, "sec": to}
        first.append(begin(remote(gram.at[place(o, to)], held.at[b - 1], send1.at[b - 1], recv1.at[b - 1], dev)))
    mine = place(o, s)
    part = gram[mine, :]
    for b in range(1, m):
        first[b - 1].wait_recv()
        part += held[b - 1]
    whole[mine, :] = part
    peers = [(i, a, b) for i, (a, b) in enumerate(others) if wide or not a]
    for i, a, b in peers:
        begin(remote(whole.at[mine], whole.at[mine], send2.at[i], recv2.at[i], devs[i]))
    for i, a, b in peers:
        at = place(lax.rem(o + n - a, n), lax.rem(s + m - b, m))
        remote(whole.at[at], whole.at[at], send2.at[i], recv2.at[i], devs[i]).wait_recv()

    block = 64
    work[:, :cols] = whole[...]
    work[:, cols:] = (
        lax.broadcasted_iota(jnp.int32, (cols, cols), 0) == lax.broadcasted_iota(jnp.int32, (cols, cols), 1)
    ).astype(jnp.float32)
    for at in range(0, cols, block):
        end = at + block
        small = small_inverse(work[at:end, at:end])
        strip = dot(small, work[at:end, :], NN, HIGHEST)
        inverse[at:end, :] = strip[:, cols:]
        if end < cols:
            work[end:, :] -= dot(strip[:, end:cols], strip, TN, HIGHEST)
    for p in range(SITE):
        part = slice(p * cols, (p + 1) * cols)
        frame[:, part] = dot(x[:, part], inverse[...], NT, HIGH)

    for k in range(pairs):
        moved = dot(left_in_block(left, o, k, scalar), frame[...], NN, HIGH)
        moved = [moved[:, q * cols:(q + 1) * cols] for q in range(SITE)]
        renorm[k] = sum(
            dot(frame[:, p * cols:(p + 1) * cols], mix_site(moved, o, k, p), TN, HIGH) for p in range(SITE)
        )
    share = taken.shape[2]

    def portion(b):
        return pl.ds(pl.multiple_of(b * share, share), share)

    third = []
    for b in range(1, m):
        to = lax.rem(s + b, m)
        dev = {"ops": o, "sec": to}
        third.append(begin(remote(renorm.at[:, portion(to)], taken.at[b - 1], send3.at[b - 1], recv3.at[b - 1], dev)))
    basis_ref[...] = frame[pl.ds(pl.multiple_of(o * row_share, row_share), row_share), :] * scale
    sector = renorm[:, portion(s), :]
    for b in range(1, m):
        third[b - 1].wait_recv()
        sector += taken[b - 1]
    summed[0] = sector
    fourth = []
    for a in range(1, n):
        dev = {"ops": lax.rem(o + a, n), "sec": s}
        fourth.append(begin(remote(summed.at[0], summed.at[a], send4.at[a - 1], recv4.at[a - 1], dev)))
    result = [jnp.zeros((share, cols), jnp.float32) for _ in range(SLOTS)]
    base = (o * SLOTS).astype(jnp.float32)
    for a in range(n):
        if a:
            fourth[a - 1].wait_recv()
        at = lax.rem(o + n - a, n)
        for k in range(pairs):
            term = summed[a, k]
            target = scalar(at, k, SITE * SITE + 1) * SLOTS + scalar(at, k, SITE * SITE + 2) - base
            for j in range(SLOTS):
                result[j] += term * (target == j).astype(jnp.float32)
    for j in range(SLOTS):
        out_ref[j] = result[j]
    for c in pending:
        c.wait_send()


def left_in_block(left, at, k, scalar):
    return left[at, k] * scalar(at, k, SITE * SITE)


def body(n, m, wavefunction, left_ops, right_ops, site_ops, pattern, sector_sizes, owner, slot):
    row_share, width = wavefunction.shape[1:]
    pairs = left_ops.shape[0]
    cols = width // SITE
    states = row_share * n
    f32 = jnp.float32
    meta = jnp.concatenate(
        [
            site_ops.reshape(pairs, SITE * SITE),
            pattern[:, :1].astype(f32),
            owner[:, None].astype(f32),
            slot[:, None].astype(f32),
        ],
        axis=1,
    )
    meta = jnp.pad(meta, ((0, 0), (0, 128 - meta.shape[1])))
    wide = cols % (8 * n * m) == 0
    rows = cols // (n * m) if wide else cols // m
    share = cols // m
    dma = pltpu.SemaphoreType.DMA
    peers = n * m - 1
    basis, complementary = pl.pallas_call(
        functools.partial(kernel, n, m, wide, float(SITE * states * m) ** 0.5),
        out_shape=[
            jax.ShapeDtypeStruct((row_share, width), f32),
            jax.ShapeDtypeStruct((SLOTS, share, cols), f32),
        ],
        in_specs=[SM, VM, ANY, ANY, ANY],
        out_specs=[VM, VM],
        scratch_shapes=[
            pltpu.VMEM((n, pairs, 128), f32),
            pltpu.VMEM((n, row_share, width), f32),
            pltpu.VMEM((n, pairs, states, states), f32),
            pltpu.VMEM((n, pairs, cols, cols), f32),
            pltpu.VMEM((n * pairs, states, width), f32),
            pltpu.VMEM((states, width), f32),
            pltpu.VMEM((cols, cols), f32),
            pltpu.VMEM((cols, cols), f32),
            pltpu.VMEM((m - 1, rows, cols), f32),
            pltpu.VMEM((cols, 2 * cols), f32),
            pltpu.VMEM((cols, cols), f32),
            pltpu.VMEM((states, width), f32),
            pltpu.VMEM((pairs, cols, cols), f32),
            pltpu.VMEM((m - 1, pairs, share, cols), f32),
            pltpu.VMEM((n, pairs, share, cols), f32),
            dma((4, n)),
            dma((4, n)),
            dma((4,)),
            dma((m - 1,)),
            dma((m - 1,)),
            dma((peers,)),
            dma((peers,)),
            dma((m - 1,)),
            dma((m - 1,)),
            dma((n - 1,)),
            dma((n - 1,)),
        ],
        compiler_params=pltpu.CompilerParams(collective_id=0, has_side_effects=True, vmem_limit_bytes=LIMIT),
    )(sector_sizes, meta, wavefunction[0], left_ops[:, 0], right_ops)
    return basis[None], complementary[None]


def solution(mesh):
    placed = (
        P("sec", "ops", None),
        P("ops", "sec", None, None),
        P("ops", None, None),
        P("ops", None, None),
        P("ops", "sec"),
        P("sec"),
        P("ops"),
        P("ops"),
    )
    return jax.shard_map(
        functools.partial(body, mesh.shape["ops"], mesh.shape["sec"]),
        mesh=mesh,
        in_specs=placed,
        out_specs=(P("sec", "ops", None), P("ops", None, "sec", None)),
        check_vma=False,
    )
```

time: 318 us -> 70.1 us (0.22)
  waiting for transfers between devices: 214 us -> 0 us
  Pallas kernels: 0 us -> 61.5 us
  other arithmetic: 58.1 us -> 0.08 us
  matrix products: 16 us -> 0 us
  between operations: 18.6 us -> 3.24 us
  local copies, waits for them, and re-layouts: 11.1 us -> 4.94 us
    psum x2 -> x0, waiting for transfers between devices: 107 us -> none  [the longest x1 70.5 us: body(): gram = lax.psum(local_gram, 'sec')]
    unnamed x6 -> x0, waiting for transfers between devices: 67.4 us -> none
    pallas_call x0 -> x1, Pallas kernels: none -> 61.5 us  [body(): pl.pallas_call(functools.partial(kernel, n, m, wide, float(SITE * states...]
    another operation x10 -> x0, other arithmetic: 53.7 us -> none  [the longest x6 34 us: body(): factor = jnp.linalg.cholesky(gram)]
    all_gather x1 -> x0, waiting for transfers between devices: 19.8 us -> none  [body(): portion = lax.all_gather(wavefunction, 'ops', axis=1, tiled=True)]
    reduce_scatter x1 -> x0, waiting for transfers between devices: 19.8 us -> none  [body(): lax.psum_scatter(routed, 'ops', scatter_dimension=0, tiled=True)]
    dot_general x7 -> x0, matrix products: 13.7 us -> none  [the longest x1 2.52 us: body(): jnp.dot(flat.T, flat, precision=highest, preferred_element_type=jnp.float32)]
    another operation x11 -> x0, local copies, waits for them, and re-layouts: 4.41 us -> none
  transfers between devices with their start and end apart: 5 -> 0, of which waited for: 5 -> 0; matrix products, arithmetic and copies ran while one was open for 1% -> 0% of each run, Pallas kernels for 0% -> 0%
where the time goes in v2:
time: 70.1 us; the launch traced here: 69.8 us
  Pallas kernels  61.5 us (88%)
  local copies, waits for them, and re-layouts  4.94 us (7%)
  between operations  3.24 us (5%)
    pallas_call x1, Pallas kernels, body(): pl.pallas_call(functools.partial(kernel, n, m, wide, float(SITE * states...  61.5 us
    unnamed x10, local copies, waits for them, and re-layouts  4.86 us

profile of v2, /device:TPU:0, one launch (start us, length us, event | category | flops | bytes accessed | tf_op | source)
XLA Modules:
  0.0 69.8 jit_solution(14016304591858899830)
XLA Ops:
  3.2 0.0 copy-start.3
  3.2 0.7 copy-done.3
  3.9 0.1 reshape.9
  4.0 0.1 select_maximum_fusion.meta_in
  4.1 0.0 copy-start
  4.1 1.0 %copy-done = f32[1,64,1024]{2,1,0:T(8,128)S(1)} copy-done((f32[1,64,1024]{2,1,0:T(8,128)S(1)}, f32[1,64,1024]{2,1,0:T(8,128)}, u32[]{:S(2)}) %copy-start) | copy-done | bytes 262168
  5.0 0.0 copy-start.1
  5.0 0.9 %copy-done.1 = f32[1,1,256,256]{3,2,1,0:T(8,128)S(1)} copy-done((f32[1,1,256,256]{3,2,1,0:T(8,128)S(1)}, f32[1,1,256,256]{3,2,1,0:T(8,128)}, u32[]{:S(2)}) %copy-start.1) | copy-done | bytes 262168
  6.0 0.0 copy-start.2
  6.0 0.9 %copy-done.2 = f32[1,256,256]{2,1,0:T(8,128)S(1)} copy-done((f32[1,256,256]{2,1,0:T(8,128)S(1)}, f32[1,256,256]{2,1,0:T(8,128)}, u32[]{:S(2)}) %copy-start.2) | copy-done | bytes 262168
  6.9 61.5 %shard_map.95 = (f32[64,1024]{1,0:T(8,128)S(1)}, f32[2,32,256]{2,1,0:T(8,128)S(1)}) custom-call(s32[1]{0:T(128)S(6)} %copy.13.size_ref, f32[1,128]{1,0:T(1,128)S(1)} %select_maximum_fusion.meta_in, f32[64,1024]{1,0:T(8,128)S(1)} %bitcast.6, f32[1,256,256]{2,1,0:T(8,128)S(1)} %bitcast.7, f32[1,256,256]{2,1,0:T(8,128)S(1)} %copy-done.2), custom_call_target="tpu_custom_call" | custom-call | tf_op jit(solution)/shard_map/pallas_call | solution.py:292
  68.4 0.7 %copy.16 = f32[1,64,1024]{2,1,0:T(8,128)} copy(f32[1,64,1024]{2,1,0:T(8,128)S(1)} %bitcast.8) | data formatting | bytes 524288
  69.2 0.6 copy.17
Async XLA Ops:
  3.2 0.7 copy-start.3
  4.1 1.0 %copy-start = (f32[1,64,1024]{2,1,0:T(8,128)S(1)}, f32[1,64,1024]{2,1,0:T(8,128)}, u32[]{:S(2)}) copy-start(f32[1,64,1024]{2,1,0:T(8,128)} %param.8) | copy-start | bytes 786436
  5.0 0.9 %copy-start.1 = (f32[1,1,256,256]{3,2,1,0:T(8,128)S(1)}, f32[1,1,256,256]{3,2,1,0:T(8,128)}, u32[]{:S(2)}) copy-start(f32[1,1,256,256]{3,2,1,0:T(8,128)} %param.9) | copy-start | bytes 786436
  6.0 0.9 %copy-start.2 = (f32[1,256,256]{2,1,0:T(8,128)S(1)}, f32[1,256,256]{2,1,0:T(8,128)}, u32[]{:S(2)}) copy-start(f32[1,256,256]{2,1,0:T(8,128)} %right_in.1) | copy-start | bytes 786436

commit v3 on v2

--- a/solution.py
+++ b/solution.py
@@ -15,7 +15,7 @@
 VM = pl.BlockSpec(memory_space=pltpu.VMEM)
 SM = pl.BlockSpec(memory_space=pltpu.SMEM)
 ANY = pl.BlockSpec(memory_space=pl.ANY)
-LIMIT = 48 * 1024 * 1024
+LIMIT = 60 * 1024 * 1024
 
 
 def remote(src, dst, send, recv, dev):
@@ -79,8 +79,8 @@
 
 def kernel(
     n, m, wide, scale, size_ref, meta_in, psi_in, left_in, right_in, basis_ref, out_ref,
-    meta, psi, left, right, mixed, x, gram, whole, held, work, inverse, frame, renorm, taken, summed,
-    send, recv, local, send1, recv1, send2, recv2, send3, recv3, send4, recv4,
+    meta, psi, left, right, mixed, x, gram, whole, held, work, inverse, frame, renorm, moved, merged, taken, summed,
+    send, recv, local, send1, recv1, send2, recv2, send3, recv3, send4, recv4, send5, recv5,
 ):
     o, s = lax.axis_index("ops"), lax.axis_index("sec")
     pairs = left_in.shape[0]
@@ -192,6 +192,8 @@
         to = lax.rem(s + b, m)
         dev = {"ops": o, "sec": to}
         first.append(begin(remote(gram.at[place(o, to)], held.at[b - 1], send1.at[b - 1], recv1.at[b - 1], dev)))
+    for k in range(pairs):
+        moved[k] = dot(left[o, k] * scalar(o, k, SITE * SITE), x[...], NN, HIGHEST)
     mine = place(o, s)
     part = gram[mine, :]
     for b in range(1, m):
@@ -201,9 +203,36 @@
     peers = [(i, a, b) for i, (a, b) in enumerate(others) if wide or not a]
     for i, a, b in peers:
         begin(remote(whole.at[mine], whole.at[mine], send2.at[i], recv2.at[i], devs[i]))
+    for k in range(pairs):
+        parts = [moved[k, :, q * cols:(q + 1) * cols] for q in range(SITE)]
+        renorm[k] = sum(
+            dot(x[:, p * cols:(p + 1) * cols], mix_site(parts, o, k, p), TN, HIGHEST) for p in range(SITE)
+        )
     for i, a, b in peers:
         at = place(lax.rem(o + n - a, n), lax.rem(s + m - b, m))
         remote(whole.at[at], whole.at[at], send2.at[i], recv2.at[i], devs[i]).wait_recv()
+
+    share = taken.shape[2]
+
+    def portion(b):
+        return pl.ds(pl.multiple_of(b * share, share), share)
+
+    ours = portion(s)
+    third = []
+    for b in range(1, m):
+        to = lax.rem(s + b, m)
+        dev = {"ops": o, "sec": to}
+        third.append(begin(remote(renorm.at[:, portion(to)], taken.at[b - 1], send3.at[b - 1], recv3.at[b - 1], dev)))
+
+    def sum_and_spread():
+        sector = renorm[:, ours, :]
+        for b in range(1, m):
+            third[b - 1].wait_recv()
+            sector += taken[b - 1]
+        merged[:, ours, :] = sector
+        for b in range(1, m):
+            dev = {"ops": o, "sec": lax.rem(s + b, m)}
+            begin(remote(merged.at[:, ours], merged.at[:, ours], send5.at[b - 1], recv5.at[b - 1], dev))
 
     block = 64
     work[:, :cols] = whole[...]
@@ -217,32 +246,20 @@
         inverse[at:end, :] = strip[:, cols:]
         if end < cols:
             work[end:, :] -= dot(strip[:, end:cols], strip, TN, HIGHEST)
+        if at == cols // 2 - block:
+            sum_and_spread()
     for p in range(SITE):
         part = slice(p * cols, (p + 1) * cols)
         frame[:, part] = dot(x[:, part], inverse[...], NT, HIGH)
 
+    basis_ref[...] = frame[pl.ds(pl.multiple_of(o * row_share, row_share), row_share), :] * scale
+
+    for b in range(1, m):
+        at = portion(lax.rem(s + m - b, m))
+        dev = {"ops": o, "sec": lax.rem(s + b, m)}
+        remote(merged.at[:, at], merged.at[:, at], send5.at[b - 1], recv5.at[b - 1], dev).wait_recv()
     for k in range(pairs):
-        moved = dot(left_in_block(left, o, k, scalar), frame[...], NN, HIGH)
-        moved = [moved[:, q * cols:(q + 1) * cols] for q in range(SITE)]
-        renorm[k] = sum(
-            dot(frame[:, p * cols:(p + 1) * cols], mix_site(moved, o, k, p), TN, HIGH) for p in range(SITE)
-        )
-    share = taken.shape[2]
-
-    def portion(b):
-        return pl.ds(pl.multiple_of(b * share, share), share)
-
-    third = []
-    for b in range(1, m):
-        to = lax.rem(s + b, m)
-        dev = {"ops": o, "sec": to}
-        third.append(begin(remote(renorm.at[:, portion(to)], taken.at[b - 1], send3.at[b - 1], recv3.at[b - 1], dev)))
-    basis_ref[...] = frame[pl.ds(pl.multiple_of(o * row_share, row_share), row_share), :] * scale
-    sector = renorm[:, portion(s), :]
-    for b in range(1, m):
-        third[b - 1].wait_recv()
-        sector += taken[b - 1]
-    summed[0] = sector
+        summed[0, k] = dot(dot(inverse[ours, :], merged[k], NN, HIGHEST), inverse[...], NT, HIGHEST)
     fourth = []
     for a in range(1, n):
         dev = {"ops": lax.rem(o + a, n), "sec": s}
@@ -262,10 +279,6 @@
         out_ref[j] = result[j]
     for c in pending:
         c.wait_send()
-
-
-def left_in_block(left, at, k, scalar):
-    return left[at, k] * scalar(at, k, SITE * SITE)
 
 
 def body(n, m, wavefunction, left_ops, right_ops, site_ops, pattern, sector_sizes, owner, slot):
@@ -311,6 +324,8 @@
             pltpu.VMEM((cols, cols), f32),
             pltpu.VMEM((states, width), f32),
             pltpu.VMEM((pairs, cols, cols), f32),
+            pltpu.VMEM((pairs, states, width), f32),
+            pltpu.VMEM((pairs, cols, cols), f32),
             pltpu.VMEM((m - 1, pairs, share, cols), f32),
             pltpu.VMEM((n, pairs, share, cols), f32),
             dma((4, n)),
@@ -324,6 +339,8 @@
             dma((m - 1,)),
             dma((n - 1,)),
             dma((n - 1,)),
+            dma((m - 1,)),
+            dma((m - 1,)),
         ],
         compiler_params=pltpu.CompilerParams(collective_id=0, has_side_effects=True, vmem_limit_bytes=LIMIT),
     )(sector_sizes, meta, wavefunction[0], left_ops[:, 0], right_ops)

time: 70.1 us -> 69.4 us (0.990)
  local copies, waits for them, and re-layouts: 4.94 us -> 3.09 us
  Pallas kernels: 61.5 us -> 62.3 us
    unnamed x10 -> x6, local copies, waits for them, and re-layouts: 4.86 us -> 3.01 us
    pallas_call x1, Pallas kernels: 61.5 us -> 62.3 us  [body(): pl.pallas_call(functools.partial(kernel, n, m, wide, float(SITE * states...]
where the time goes in v3:
time: 69.4 us; the launch traced here: 69.2 us
  Pallas kernels  62.3 us (90%)
  between operations  3.24 us (5%)
  local copies, waits for them, and re-layouts  3.09 us (4%)
    pallas_call x1, Pallas kernels, body(): pl.pallas_call(functools.partial(kernel, n, m, wide, float(SITE * states...  62.3 us
    unnamed x6, local copies, waits for them, and re-layouts  3.01 us

profile of v3, /device:TPU:0, one launch (start us, length us, event | category | flops | bytes accessed | tf_op | source)
XLA Modules:
  0.0 69.2 jit_solution(2269146161296066168)
XLA Ops:
  3.2 0.0 copy-start.1
  3.2 0.7 copy-done.1
  3.9 0.1 reshape.9
  4.0 0.6 select_maximum_fusion.meta_in
  4.6 62.3 %shard_map.95 = (f32[64,1024]{1,0:T(8,128)}, f32[2,32,256]{2,1,0:T(8,128)}) custom-call(s32[1]{0:T(128)S(6)} %copy.13.size_ref, f32[1,128]{1,0:T(1,128)} %select_maximum_fusion.meta_in, f32[64,1024]{1,0:T(8,128)} %bitcast.6, f32[1,256,256]{2,1,0:T(8,128)} %bitcast.7, f32[1,256,256]{2,1,0:T(8,128)} %right_in.1), custom_call_target="tpu_custom_call" | custom-call | tf_op jit(solution)/shard_map/pallas_call | solution.py:305
  66.9 0.0 copy-start
  66.9 1.7 %copy.16 = f32[1,64,1024]{2,1,0:T(8,128)} copy(f32[1,64,1024]{2,1,0:T(8,128)} %bitcast.8) | data formatting | bytes 524288
  68.6 0.0 copy-done
  68.6 0.6 copy.17
Async XLA Ops:
  3.2 0.7 copy-start.1
  66.9 1.7 %copy-start = (f32[2,32,256]{2,1,0:T(8,128)S(1)}, f32[2,32,256]{2,1,0:T(8,128)}, u32[]{:S(2)}) copy-start(f32[2,32,256]{2,1,0:T(8,128)} %get-tuple-element.5) | copy-start | bytes 196612

commit v4 on v3

--- a/solution.py
+++ b/solution.py
@@ -78,16 +78,16 @@
 
 
 def kernel(
-    n, m, wide, scale, size_ref, meta_in, psi_in, left_in, right_in, basis_ref, out_ref,
+    n, m, wide, size_ref, meta_in, psi_in, left_in, right_in, basis_ref, out_ref,
     meta, psi, left, right, mixed, x, gram, whole, held, work, inverse, frame, renorm, moved, merged, taken, summed,
-    send, recv, local, send1, recv1, send2, recv2, send3, recv3, send4, recv4, send5, recv5,
+    send, recv, local, send1, recv1, send2, recv2, send3, recv3, send4, recv4, send5, recv5, send6, recv6,
 ):
     o, s = lax.axis_index("ops"), lax.axis_index("sec")
     pairs = left_in.shape[0]
     row_share, width = psi_in.shape
     states = row_share * n
     cols = width // SITE
-    others = [(a, b) for a in range(n) for b in range(m) if (a or b) and (wide or not a or not b)]
+    others = [(a, b) for a in range(n) for b in range(m) if (a or b) and not (a and b)]
     devs = [{"ops": lax.rem(o + a, n), "sec": lax.rem(s + b, m)} for a, b in others]
     greet(devs)
 
@@ -101,6 +101,11 @@
     away = [{"ops": lax.rem(chip + d, chips) * 2 + core, "sec": s} for d in range(1, chips)]
     back = [lax.rem(chip + chips - d, chips) * 2 + core for d in range(1, chips)]
     far = [lax.rem(chip + chips - d, chips) * 2 + 1 - core for d in range(1, chips)]
+    side = lax.rem(s, 2)
+    half = cols // 2
+    ours_half = pl.ds(pl.multiple_of(side * half, half), half)
+    other_half = pl.ds(pl.multiple_of((1 - side) * half, half), half)
+    twin = {"ops": o, "sec": s + 1 - 2 * side}
     pending = []
 
     def begin(c):
@@ -111,7 +116,10 @@
     own = [pltpu.make_async_copy(ins[a], outs[a].at[o], local.at[a]) for a in range(4)]
     for a in range(4):
         for i, dev in enumerate(away):
-            begin(remote(ins[a], outs[a].at[o], send.at[a, i], recv.at[a, i], dev))
+            if a == 2:
+                begin(remote(right_in.at[:, ours_half], right.at[o, :, ours_half], send.at[a, i], recv.at[a, i], dev))
+            else:
+                begin(remote(ins[a], outs[a].at[o], send.at[a, i], recv.at[a, i], dev))
         begin(remote(ins[a], outs[a].at[o], send.at[a, direct], recv.at[a, direct], mate))
         own[a].start()
 
@@ -119,6 +127,23 @@
         for i, src in enumerate(back):
             remote(ins[a], outs[a].at[src], send.at[a, i], recv.at[a, i], away[i]).wait_recv()
             begin(remote(outs[a].at[src], outs[a].at[src], send.at[a, chips + i], recv.at[a, chips + i], mate))
+
+    def relay_right():
+        for i, src in enumerate(back):
+            here = right.at[src, :, ours_half]
+            remote(here, here, send.at[2, i], recv.at[2, i], away[i]).wait_recv()
+            begin(remote(here, here, send6.at[i], recv6.at[i], twin))
+            begin(remote(here, here, send.at[2, chips + i], recv.at[2, chips + i], mate))
+        for i, src in enumerate(back):
+            here = right.at[src, :, other_half]
+            remote(here, here, send6.at[i], recv6.at[i], twin).wait_recv()
+            begin(remote(here, here, send6.at[chips + i], recv6.at[chips + i], mate))
+
+    def far_right(i):
+        here = right.at[far[i], :, ours_half]
+        remote(here, here, send.at[2, chips + i], recv.at[2, chips + i], mate).wait_recv()
+        here = right.at[far[i], :, other_half]
+        remote(here, here, send6.at[chips + i], recv6.at[chips + i], mate).wait_recv()
 
     def from_mate(a):
         remote(ins[a], outs[a].at[mate_at], send.at[a, direct], recv.at[a, direct], mate).wait_recv()
@@ -167,7 +192,9 @@
             from_mate(a)
         elif i < 2 + direct:
             if i == 2:
-                relay(a)
+                relay_right() if a == 2 else relay(a)
+        elif a == 2:
+            far_right(i - 2 - direct)
         else:
             from_far(a, i - 2 - direct)
 
@@ -179,7 +206,7 @@
         arrive(3, i)
         total = apply_left(i, total)
     x[...] = jnp.where(live, total, 0.0)
-    gram[...] = sum(dot(x[:, p * cols:(p + 1) * cols], x[:, p * cols:(p + 1) * cols], TN, HIGHEST) for p in range(SITE))
+    gram[...] = sum(dot(x[:, p * cols:(p + 1) * cols], x[:, p * cols:(p + 1) * cols], TN, HIGH) for p in range(SITE))
 
     rows = held.shape[1]
 
@@ -200,17 +227,23 @@
         first[b - 1].wait_recv()
         part += held[b - 1]
     whole[mine, :] = part
-    peers = [(i, a, b) for i, (a, b) in enumerate(others) if wide or not a]
-    for i, a, b in peers:
-        begin(remote(whole.at[mine], whole.at[mine], send2.at[i], recv2.at[i], devs[i]))
+    for b in range(1, m):
+        dev = {"ops": o, "sec": lax.rem(s + b, m)}
+        begin(remote(whole.at[mine], whole.at[mine], send2.at[b - 1], recv2.at[b - 1], dev))
+    for b in range(m):
+        at = place(o, lax.rem(s + m - b, m))
+        if b:
+            dev = {"ops": o, "sec": lax.rem(s + b, m)}
+            remote(whole.at[at], whole.at[at], send2.at[b - 1], recv2.at[b - 1], dev).wait_recv()
+        for a in range(1, n if wide else 1):
+            i = a * m - 1 + b
+            dev = {"ops": lax.rem(o + a, n), "sec": s}
+            begin(remote(whole.at[at], whole.at[at], send2.at[i], recv2.at[i], dev))
     for k in range(pairs):
         parts = [moved[k, :, q * cols:(q + 1) * cols] for q in range(SITE)]
         renorm[k] = sum(
             dot(x[:, p * cols:(p + 1) * cols], mix_site(parts, o, k, p), TN, HIGHEST) for p in range(SITE)
         )
-    for i, a, b in peers:
-        at = place(lax.rem(o + n - a, n), lax.rem(s + m - b, m))
-        remote(whole.at[at], whole.at[at], send2.at[i], recv2.at[i], devs[i]).wait_recv()
 
     share = taken.shape[2]
 
@@ -223,6 +256,12 @@
         to = lax.rem(s + b, m)
         dev = {"ops": o, "sec": to}
         third.append(begin(remote(renorm.at[:, portion(to)], taken.at[b - 1], send3.at[b - 1], recv3.at[b - 1], dev)))
+    for a in range(1, n if wide else 1):
+        for b in range(m):
+            i = a * m - 1 + b
+            at = place(lax.rem(o + n - a, n), lax.rem(s + m - b, m))
+            dev = {"ops": lax.rem(o + a, n), "sec": s}
+            remote(whole.at[at], whole.at[at], send2.at[i], recv2.at[i], dev).wait_recv()
 
     def sum_and_spread():
         sector = renorm[:, ours, :]
@@ -245,14 +284,14 @@
         strip = dot(small, work[at:end, :], NN, HIGHEST)
         inverse[at:end, :] = strip[:, cols:]
         if end < cols:
-            work[end:, :] -= dot(strip[:, end:cols], strip, TN, HIGHEST)
+            work[end:, :] -= dot(strip[:, end:cols], strip, TN, HIGH)
         if at == cols // 2 - block:
             sum_and_spread()
     for p in range(SITE):
         part = slice(p * cols, (p + 1) * cols)
         frame[:, part] = dot(x[:, part], inverse[...], NT, HIGH)
 
-    basis_ref[...] = frame[pl.ds(pl.multiple_of(o * row_share, row_share), row_share), :] * scale
+    basis_ref[...] = frame[pl.ds(pl.multiple_of(o * row_share, row_share), row_share), :]
 
     for b in range(1, m):
         at = portion(lax.rem(s + m - b, m))
@@ -303,7 +342,7 @@
     dma = pltpu.SemaphoreType.DMA
     peers = n * m - 1
     basis, complementary = pl.pallas_call(
-        functools.partial(kernel, n, m, wide, float(SITE * states * m) ** 0.5),
+        functools.partial(kernel, n, m, wide),
         out_shape=[
             jax.ShapeDtypeStruct((row_share, width), f32),
             jax.ShapeDtypeStruct((SLOTS, share, cols), f32),
@@ -341,10 +380,12 @@
             dma((n - 1,)),
             dma((m - 1,)),
             dma((m - 1,)),
+            dma((n,)),
+            dma((n,)),
         ],
         compiler_params=pltpu.CompilerParams(collective_id=0, has_side_effects=True, vmem_limit_bytes=LIMIT),
     )(sector_sizes, meta, wavefunction[0], left_ops[:, 0], right_ops)
-    return basis[None], complementary[None]
+    return (basis * (float(SITE * states * m) ** 0.5))[None], complementary[None]
 
 
 def solution(mesh):

time: 69.4 us -> 65.8 us (0.948)
  Pallas kernels: 62.3 us -> 58.6 us
  other arithmetic: 0.63 us -> 2.33 us
  local copies, waits for them, and re-layouts: 3.09 us -> 1.39 us
    pallas_call x1, Pallas kernels: 62.3 us -> 58.6 us  [body(): pl.pallas_call(functools.partial(kernel, n, m, wide), out_shape=[jax.Shap...]
    broadcast_in_dim x0 -> x1, other arithmetic: none -> 1.71 us  [body(): (basis * float(SITE * states * m) ** 0.5)[None]]
    unnamed x6 -> x5, local copies, waits for them, and re-layouts: 3.01 us -> 1.31 us
where the time goes in v4:
time: 65.8 us; the launch traced here: 65.6 us
  Pallas kernels  58.6 us (89%)
  between operations  3.24 us (5%)
  other arithmetic  2.33 us (4%)
  local copies, waits for them, and re-layouts  1.39 us (2%)
    pallas_call x1, Pallas kernels, body(): pl.pallas_call(functools.partial(kernel, n, m, wide), out_shape=[jax.Shap...  58.6 us
    broadcast_in_dim x1, other arithmetic, body(): (basis * float(SITE * states * m) ** 0.5)[None]  1.71 us

profile of v4, /device:TPU:0, one launch (start us, length us, event | category | flops | bytes accessed | tf_op | source)
XLA Modules:
  0.0 65.6 jit_solution(16551439759913733010)
XLA Ops:
  3.2 0.0 copy-start.1
  3.2 0.7 %copy-done.1 = f32[1,4,4]{2,1,0:T(4,128)S(1)} copy-done((f32[1,4,4]{2,1,0:T(4,128)S(1)}, f32[1,4,4]{2,1,0:T(4,128)}, u32[]{:S(2)}) %copy-start.1) | copy-done | bytes 88
  3.9 0.1 reshape.9
  4.0 0.6 select_maximum_fusion.meta_in
  4.6 58.6 %shard_map.95 = (f32[64,1024]{1,0:T(8,128)}, f32[2,32,256]{2,1,0:T(8,128)}) custom-call(s32[1]{0:T(128)S(6)} %copy.12.size_ref, f32[1,128]{1,0:T(1,128)} %select_maximum_fusion.meta_in, f32[64,1024]{1,0:T(8,128)} %bitcast.7, f32[1,256,256]{2,1,0:T(8,128)} %bitcast.8, f32[1,256,256]{2,1,0:T(8,128)} %right_in.1), custom_call_target="tpu_custom_call" | custom-call | tf_op jit(solution)/shard_map/pallas_call | solution.py:344
  63.2 0.0 copy-start
  63.2 1.7 %multiply_bitcast_fusion = f32[1,64,1024]{2,1,0:T(8,128)} fusion(f32[64,1024]{1,0:T(8,128)} %get-tuple-element.4), kind=kLoop, calls=%fused_computation | loop fusion | flops 65536 | bytes 524288 | tf_op jit(solution)/shard_map/broadcast_in_dim | solution.py:388
  64.9 0.0 copy-done
  64.9 0.6 copy.15
Async XLA Ops:
  3.2 0.7 %copy-start.1 = (f32[1,4,4]{2,1,0:T(4,128)S(1)}, f32[1,4,4]{2,1,0:T(4,128)}, u32[]{:S(2)}) copy-start(f32[1,4,4]{2,1,0:T(4,128)} %param.11) | copy-start | bytes 196
  63.2 1.7 %copy-start = (f32[2,32,256]{2,1,0:T(8,128)S(1)}, f32[2,32,256]{2,1,0:T(8,128)}, u32[]{:S(2)}) copy-start(f32[2,32,256]{2,1,0:T(8,128)} %get-tuple-element.5) | copy-start | bytes 196612

commit v5 on v4

--- a/solution.py
+++ b/solution.py
@@ -57,9 +57,13 @@
         ]
         rows = parts[g]
         for r in range(8):
-            inv = 1.0 / spread[0][r][r:r + 1, :]
+            pivot = spread[0][r][r:r + 1, :]
+            inv = pl.reciprocal(pivot, approx=True)
+            inv = inv * (2.0 - pivot * inv)
+            inv = inv * (2.0 - pivot * inv)
             ratio = rows[r:r + 1, :] * inv
-            steps = [spread[0][i][r:r + 1, :] * inv for i in range(r + 1, 8)]
+            above = [spread[0][i][r:r + 1, :] for i in range(r + 1, 8)]
+            steps = [a * inv for a in above]
             for t in range(count - g):
                 col = spread[t][r]
                 if t == 0:
@@ -70,7 +74,10 @@
                 else:
                     parts[g + t] = parts[g + t] - col * ratio
                 for i in range(r + 1, 8):
-                    spread[t][i] = spread[t][i] - col * steps[i - r - 1]
+                    if t == 0:
+                        spread[t][i] = spread[t][i] - (col * above[i - r - 1]) * inv
+                    else:
+                        spread[t][i] = spread[t][i] - col * steps[i - r - 1]
         parts[g] = rows
     work = jnp.concatenate(parts, axis=0)
     pivot = jnp.sum(work[:, :b] * eye, axis=1, keepdims=True)

time: 65.8 us -> 68.3 us (1.038)
  Pallas kernels: 58.6 us -> 61.2 us
    pallas_call x1, Pallas kernels: 58.6 us -> 61.2 us  [body(): pl.pallas_call(functools.partial(kernel, n, m, wide), out_shape=[jax.Shap...]
where the time goes in v5:
time: 68.3 us; the launch traced here: 68.1 us
  Pallas kernels  61.2 us (90%)
  between operations  3.24 us (5%)
  other arithmetic  2.33 us (3%)
  local copies, waits for them, and re-layouts  1.39 us (2%)
    pallas_call x1, Pallas kernels, body(): pl.pallas_call(functools.partial(kernel, n, m, wide), out_shape=[jax.Shap...  61.2 us
    broadcast_in_dim x1, other arithmetic, body(): (basis * float(SITE * states * m) ** 0.5)[None]  1.71 us

profile of v5, /device:TPU:0, one launch (start us, length us, event | category | flops | bytes accessed | tf_op | source)
XLA Modules:
  0.0 68.1 jit_solution(1241322296608252973)
XLA Ops:
  3.2 0.0 copy-start.1
  3.2 0.7 copy-done.1
  3.9 0.1 reshape.9
  4.0 0.6 select_maximum_fusion.meta_in
  4.6 61.2 %shard_map.95 = (f32[64,1024]{1,0:T(8,128)}, f32[2,32,256]{2,1,0:T(8,128)}) custom-call(s32[1]{0:T(128)S(6)} %copy.12.size_ref, f32[1,128]{1,0:T(1,128)} %select_maximum_fusion.meta_in, f32[64,1024]{1,0:T(8,128)} %bitcast.7, f32[1,256,256]{2,1,0:T(8,128)} %bitcast.8, f32[1,256,256]{2,1,0:T(8,128)} %right_in.1), custom_call_target="tpu_custom_call" | custom-call | tf_op jit(solution)/shard_map/pallas_call | solution.py:351
  65.8 0.0 copy-start
  65.8 1.7 %multiply_bitcast_fusion = f32[1,64,1024]{2,1,0:T(8,128)} fusion(f32[64,1024]{1,0:T(8,128)} %get-tuple-element.4), kind=kLoop, calls=%fused_computation | loop fusion | flops 65536 | bytes 524288 | tf_op jit(solution)/shard_map/broadcast_in_dim | solution.py:395
  67.5 0.0 copy-done
  67.5 0.6 copy.15
Async XLA Ops:
  3.2 0.7 %copy-start.1 = (f32[1,4,4]{2,1,0:T(4,128)S(1)}, f32[1,4,4]{2,1,0:T(4,128)}, u32[]{:S(2)}) copy-start(f32[1,4,4]{2,1,0:T(4,128)} %param.11) | copy-start | bytes 196
  65.8 1.7 %copy-start = (f32[2,32,256]{2,1,0:T(8,128)S(1)}, f32[2,32,256]{2,1,0:T(8,128)}, u32[]{:S(2)}) copy-start(f32[2,32,256]{2,1,0:T(8,128)} %get-tuple-element.5) | copy-start | bytes 196612
